TPU v7x, 32 devices: a whole 2x2x4 slice. The times are simulated.
32 devices in a mesh: dp: 8 (over z, y), seq: 4 (over x, core).
Axes of the slice: x: 2, y: 2, z: 4, core: 2. Of those that a mesh axis runs over, the one named last changes fastest.
Arguments:
- inputs: bfloat16 [8, 1536, 1024], P('dp', 'seq'), may hold values from -6 to 6
- conv_weight: bfloat16 [1024, 3, 384], P(('dp', 'seq')), may hold values from -0.109375 to 0.109375
- out_weight: bfloat16 [1024, 384], P(('dp', 'seq')), may hold values from -0.3125 to 0.3125
- cotangent: bfloat16 [8, 1536, 1024], P('dp', 'seq'), may hold values from -8 to 8
Outputs:
- outputs: bfloat16 [8, 1536, 1024], P('dp', 'seq')
- input_grad: bfloat16 [8, 1536, 1024], P('dp', 'seq')
- conv_grad: float32 [1024, 3, 384], P(('dp', 'seq'))
- out_grad: float32 [1024, 384], P(('dp', 'seq'))
All inputs are finite; a program needn't handle non-finite values.
Results may differ from a plain program's by a relative error of at most 0.009.
Values may be sent and summed in bfloat16 or wider, within the bound.
A program may use at most 64 MiB of HBM per device.

v0:
```python
import math

import jax
import jax.numpy as jnp
from jax import lax
from jax.sharding import PartitionSpec as P


def with_halo(cells, sides, width):
    for axis, dim in sides:
        count = lax.axis_size(axis)
        ends = count - 1
        head = lax.slice_in_dim(cells, 0, width, axis=dim)
        tail = lax.slice_in_dim(cells, cells.shape[dim] - width, cells.shape[dim], axis=dim)
        cells = jnp.concatenate(
            [
                lax.ppermute(tail, axis, [(i, (i + 1) % count) for i in range(ends)]),
                cells,
                lax.ppermute(head, axis, [((i + 1) % count, i) for i in range(ends)]),
            ],
            axis=dim,
        )
    return cells


def shards(inputs, conv_weight, out_weight, cotangent):
    input_rows = inputs.shape[1]
    chans = inputs.shape[2]
    dilation_gap = input_rows // 2
    source = inputs[0]
    upstream = cotangent[0]
    wconv, wout = (
        lax.all_gather(conv_weight, ("dp", "seq"), axis=0, tiled=True),
        lax.all_gather(out_weight, ("dp", "seq"), axis=0, tiled=True),
    )
    hidden = wout.shape[1]
    wflat = wconv.reshape(chans, 3 * hidden)
    activated_value = jax.nn.gelu(source.astype(jnp.float32)).astype(jnp.bfloat16)
    widened_input = with_halo(activated_value, (("seq", 0),), dilation_gap)
    pre = jnp.zeros((input_rows, hidden), jnp.float32)
    for kernel_offset in range(3):
        piece = jnp.dot(
            widened_input[kernel_offset * dilation_gap : kernel_offset * dilation_gap + input_rows],
            wconv[:, kernel_offset, :],
            preferred_element_type=jnp.float32,
        )
        pre = pre + piece.astype(jnp.bfloat16).astype(jnp.float32)
    mid = jax.nn.gelu(pre).astype(jnp.bfloat16)
    outputs = (
        source.astype(jnp.float32) + jnp.dot(mid, wout.T, preferred_element_type=jnp.float32)
    ).astype(jnp.bfloat16)
    dmid = jnp.dot(upstream, wout, preferred_element_type=jnp.float32)
    preactivation_gradient = jax.vjp(jax.nn.gelu, pre)[1](dmid)[0].astype(jnp.bfloat16)
    zero_bordered = with_halo(preactivation_gradient, (("seq", 0),), dilation_gap)
    offset_input = jnp.concatenate(
        [
            zero_bordered[2 * dilation_gap : 2 * dilation_gap + input_rows],
            zero_bordered[dilation_gap : dilation_gap + input_rows],
            zero_bordered[:input_rows],
        ],
        axis=1,
    )
    dact = jnp.dot(offset_input, wflat.T, preferred_element_type=jnp.float32)
    factor = 1.0 / math.sqrt(input_rows * lax.axis_size("seq") * lax.axis_size("dp"))
    conv_part = (
        jnp.einsum("pc,pk->ck", activated_value, offset_input, preferred_element_type=jnp.float32)
        * factor
    ).reshape(chans, 3, hidden)
    out_part = jnp.einsum("pc,ph->ch", upstream, mid, preferred_element_type=jnp.float32) * factor
    input_grad = (
        upstream.astype(jnp.float32) + jax.vjp(jax.nn.gelu, source.astype(jnp.float32))[1](dact)[0]
    ).astype(jnp.bfloat16)
    conv_grad, out_grad = (
        lax.psum_scatter(conv_part, ("dp", "seq"), scatter_dimension=0, tiled=True),
        lax.psum_scatter(out_part, ("dp", "seq"), scatter_dimension=0, tiled=True),
    )
    return (outputs[None], input_grad[None], conv_grad, out_grad)


def solution(mesh):
    return jax.shard_map(
        shards,
        mesh=mesh,
        in_specs=(
            P("dp", "seq", None),
            P(("dp", "seq"), None, None),
            P(("dp", "seq"), None),
            P("dp", "seq", None),
        ),
        out_specs=(
            P("dp", "seq", None),
            P("dp", "seq", None),
            P(("dp", "seq"), None, None),
            P(("dp", "seq"), None),
        ),
        check_vma=False,
    )
```

profile of v0, /device:TPU:0, one launch (start us, length us, event | category | flops | bytes accessed | tf_op | source)
XLA Modules:
  0.0 370.1 jit_solution(5287647074932074410)
XLA Ops:
  8.0 1.7 fusion.14
  9.6 0.8 fusion.67
  10.4 1.3 collective-permute-start.1
  11.7 3.8 %collective-permute-start = (bf16[192,1024]{1,0:T(8,128)(2,1)}, bf16[192,1024]{1,0:T(8,128)(2,1)}, u32[]{:S(2)}, u32[]{:S(2)}) collective-permute-start(bf16[192,1024]{1,0:T(8,128)(2,1)} %get-tuple-element.17), channel_id=1, source_target_pairs={{0,1},{1,2},{2,3},{4,5},{5,6},{6,7},{8,9},{9,10},{10,11},{12,13},{... | collective-permute-start | bytes 1179656 | tf_op jit(solution)/shard_map/ppermute | solution.py:17
  15.5 48.5 %all_gather.7 = bf16[1024,384]{1,0:T(8,128)(2,1)} all-gather(bf16[32,384]{1,0:T(8,128)(2,1)S(1)} %copy-done.4), channel_id=1, replica_groups=mesh['dp'=8,'seq'=4] {'dp','seq'}, dimensions={0}, use_global_device_ids=true | all-gather | bytes 811008 | tf_op jit(solution)/shard_map/all_gather | solution.py:34
  64.0 7.4 %all-gather.2.cloned.1.call-done = bf16[1024,3,384]{2,0,1:T(8,128)(2,1)} async-done(((bf16[32,3,384]{2,0,1:T(8,128)(2,1)}), bf16[1024,3,384]{2,0,1:T(8,128)(2,1)}) %all-gather.2.cloned.1.call-update) | async-done | bytes 2359312 | tf_op jit(solution)/shard_map/all_gather | solution.py:33
  71.3 2.2 fusion.27
  73.6 1.6 fusion.29
  75.2 1.7 fusion.26
  77.0 0.8 fusion.50
  77.8 1.3 collective-permute-start.2
  79.1 3.0 collective-permute-start.3
  82.2 1.0 collective-permute-done.3
  83.8 3.8 %convolution_multiply_fusion = f32[1024,1152]{1,0:T(8,128)} fusion(bf16[384,384]{1,0:T(8,128)(2,1)S(1)} %fusion.50, bf16[192,384]{1,0:T(8,128)(2,1)S(1)} %collective-permute-done.3, bf16[192,384]{1,0:T(8,128)(2,1)S(1)} %collective-permute-done.2, bf16[1,384,1024]{2,1,0:T(8,128)(2,1)S(1)} %copy-done.2), kind=kOutput, calls=%fused_computation | convolution fusion | flops 915505152 | bytes 6094848 | tf_op jit(solution)/shard_map/pc,pk->ck/dot_general | solution.py:66
  87.6 6.0 %copy.15 = f32[1024,1152]{0,1:T(8,128)} copy(f32[1024,1152]{1,0:T(8,128)} %convolution_multiply_fusion) | data formatting | bytes 9437184 | tf_op jit(solution)/shard_map/mul | solution.py:66
  93.7 7.2 %copy.16 = f32[1024,3,384]{2,1,0:T(4,128)} copy(f32[1024,3,384]{0,2,1:T(8,128)} %bitcast.87) | data formatting | bytes 9437184 | tf_op jit(solution)/shard_map/reshape | solution.py:68
  100.9 3.2 multiply_bitcast_fusion
  104.1 3.0 copy.19
  107.2 2.6 copy.14
  109.7 3.0 fusion.24
  112.8 3.9 %fusion.43 = bf16[1,384,1024]{2,1,0:T(8,128)(2,1)} fusion(bf16[1,384,1024]{2,1,0:T(8,128)(2,1)S(1)} %copy-done.2, bf16[1,384,1024]{2,1,0:T(8,128)(2,1)S(1)} %copy-done.6, bf16[1024,1152]{0,1:T(8,128)(2,1)S(1)} %bitcast.88, bf16[384,384]{1,0:T(8,128)(2,1)S(1)} %fusion.50, bf16[192,384]{1,0:T(8,128)(2,1)} %copy-done.8, bf16[192,384]{1,0:T(8,128)(2,1)} %copy-done.7), kind=kOutput, calls=%fused_computation.61 | convolution fusion | flops 919437312 | bytes 5308416 | tf_op jit(solution)/shard_map/dot_general | solution.py:63
  116.7 143.3 %all-reduce.3.cloned.1.call-done = f32[1024,3,384]{2,1,0:T(4,128)} async-done(((f32[1024,3,384]{2,1,0:T(4,128)}), f32[1024,3,384]{2,1,0:T(4,128)}) %all-reduce.3.cloned.1.call-update) | async-done | bytes 4718608
  260.0 1.0 constant_dynamic-slice_fusion
  261.7 101.9 %reduce-scatter.4.cloned.1.call-done = f32[32,384]{1,0:T(8,128)} async-done(((f32[1024,384]{1,0:T(8,128)}), f32[32,384]{1,0:T(8,128)}) %reduce-scatter.4.cloned.1.call-update) | async-done | bytes 49168
  (31 shorter events, 2.2 us)
Async XLA Ops:
  7.2 64.2 %all-gather.2.cloned.1.call-start = ((), (), s32[]{:S(2)}) async-start(), calls=%async_computation.1 | async-start | bytes 2433024 | tf_op jit(solution)/shard_map/all_gather | solution.py:33
  7.9 7.6 %copy-start.4 = (bf16[32,384]{1,0:T(8,128)(2,1)S(1)}, bf16[32,384]{1,0:T(8,128)(2,1)}, u32[]{:S(2)}) copy-start(bf16[32,384]{1,0:T(8,128)(2,1)} %param.6) | copy-start | bytes 73732
  7.9 252.1 %all-reduce.3.cloned.1.call-start = ((), (), s32[]{:S(2)}) async-start(), calls=%async_computation.3 | async-start | bytes 12582912
  10.4 64.8 %collective-permute-start.1 = (bf16[192,1024]{1,0:T(8,128)(2,1)S(1)}, bf16[192,1024]{1,0:T(8,128)(2,1)}, u32[]{:S(2)}, u32[]{:S(2)}) collective-permute-start(bf16[192,1024]{1,0:T(8,128)(2,1)S(1)} %get-tuple-element.16), channel_id=1, source_target_pairs={{1,0},{2,1},{3,2},{5,4},{6,5},{7,6},{9,8},{10,9},{11,10},{13,12},{... | collective-permute-start | bytes 1179656 | tf_op jit(solution)/shard_map/ppermute | solution.py:19
  11.7 61.9 %collective-permute-start = (bf16[192,1024]{1,0:T(8,128)(2,1)}, bf16[192,1024]{1,0:T(8,128)(2,1)}, u32[]{:S(2)}, u32[]{:S(2)}) collective-permute-start(bf16[192,1024]{1,0:T(8,128)(2,1)} %get-tuple-element.17), channel_id=1, source_target_pairs={{0,1},{1,2},{2,3},{4,5},{5,6},{6,7},{8,9},{9,10},{10,11},{12,13},{... | collective-permute-start | bytes 1179656 | tf_op jit(solution)/shard_map/ppermute | solution.py:17
  71.3 2.2 copy-start
  75.2 1.7 copy-start.3
  75.2 1.7 copy-start.5
  76.9 0.8 copy-start.9
  76.9 6.9 %copy-start.2 = (bf16[1,384,1024]{2,1,0:T(8,128)(2,1)S(1)}, bf16[1,384,1024]{2,1,0:T(8,128)(2,1)}, u32[]{:S(2)}) copy-start(bf16[1,384,1024]{2,1,0:T(8,128)(2,1)} %param.4) | copy-start | bytes 2359300
  77.8 4.3 %collective-permute-start.2 = (bf16[192,384]{1,0:T(8,128)(2,1)S(1)}, bf16[192,384]{1,0:T(8,128)(2,1)S(1)}, u32[]{:S(2)}, u32[]{:S(2)}) collective-permute-start(bf16[192,384]{1,0:T(8,128)(2,1)S(1)} %get-tuple-element.18), channel_id=1, source_target_pairs={{1,0},{2,1},{3,2},{5,4},{6,5},{7,6},{9,8},{10,9},{11,10},{13,12},{... | collective-permute-start | bytes 442376 | tf_op jit(solution)/shard_map/ppermute | solution.py:19
  79.1 4.0 %collective-permute-start.3 = (bf16[192,384]{1,0:T(8,128)(2,1)S(1)}, bf16[192,384]{1,0:T(8,128)(2,1)S(1)}, u32[]{:S(2)}, u32[]{:S(2)}) collective-permute-start(bf16[192,384]{1,0:T(8,128)(2,1)S(1)} %get-tuple-element.19), channel_id=1, source_target_pairs={{0,1},{1,2},{2,3},{4,5},{5,6},{6,7},{8,9},{9,10},{10,11},{12,13},{... | collective-permute-start | bytes 442376 | tf_op jit(solution)/shard_map/ppermute | solution.py:17
  82.2 1.0 copy-start.7
  83.1 0.7 copy-start.8
  100.9 262.7 %reduce-scatter.4.cloned.1.call-start = ((), (), s32[]{:S(2)}) async-start(), calls=%async_computation.2 | async-start | bytes 1622016
  109.7 3.0 copy-start.1
  109.7 3.0 copy-start.6
Sparse Core Ops, SparseCore 0:
  10.8 60.4 all-gather.1
  101.0 159.0 all-reduce.2
  266.7 96.8 reduce-scatter.3
where the time goes:
time: 371 us; the launch traced here: 370 us
  waiting for transfers between devices  254 us (68%)
  blocking collectives  48.5 us (13%)
  local copies, waits for them, and re-layouts  22 us (6%)
  matrix products  20.3 us (5%)
  between operations  13.9 us (4%)
  starting transfers between devices  9.53 us (3%)
    unnamed x5, waiting for transfers between devices  246 us
    all_gather x1, blocking collectives, shards(): lax.all_gather(out_weight, ('dp', 'seq'), axis=0, tiled=True)  48.5 us
  transfers between devices with their start and end apart: 7, of which 4 were waited for; matrix products, arithmetic and copies ran while one was open for 6% of the time, Pallas kernels for 0%

commit v1 on v0

v1 whole, which is shorter than its diff:
```python
import functools
import math

import jax
import jax.numpy as jnp
from jax import lax
from jax.experimental import pallas as pl
from jax.experimental.pallas import tpu as pltpu
from jax.sharding import PartitionSpec as P

F32 = jnp.float32
BF16 = jnp.bfloat16
ALPHA = math.sqrt(2.0 / math.pi)
BETA = 0.044715


def gelu_and_slope(x):
    x2 = x * x
    t = jnp.tanh(ALPHA * x * (1.0 + BETA * x2))
    half = 0.5 * (1.0 + t)
    slope = half + 0.5 * x * (1.0 - t * t) * (ALPHA * (1.0 + 3.0 * BETA * x2))
    return x * half, slope


def gelu_only(x):
    t = jnp.tanh(ALPHA * x * (1.0 + BETA * (x * x)))
    return x * (0.5 * (1.0 + t))


def block_kernel(
    planes, factor,
    in_ref, cot_ref, w_ref,
    out_ref, ig_ref, cg_ref,
    gat, xh, act, acc, mid, dpre, dacc, part, s0, s1a, s1b, s2,
    sb0, rb0, sb1a, rb1a, sb1b, rb1b, sb2a, rb2a, sb2b, rb2b, sb3, rb3,
    gz, gax, gay, gbx, gby, gc, hx, hd, q0, q1a, q1b, q2a, q2b, q3, qloc,
):
    dp = lax.axis_index("dp")
    seq = lax.axis_index("seq")
    z, y = dp // 2, dp % 2
    x, c = seq // 2, seq % 2
    oy, ox, oc = 1 - y, 1 - x, 1 - c
    rows, chans = in_ref.shape
    gap = rows // 2
    cz = chans // planes
    hidden = w_ref.shape[2]
    seqs = 4
    ypeer = (z * 2 + oy, seq)
    xpeer = (dp, ox * 2 + c)
    cpeer = (dp, x * 2 + oc)
    diag = (dp, ox * 2 + oc)

    def zpeer(d):
        return (lax.rem(z + d, planes) * 2 + y, seq)

    def copy(src, dst, sems, peer):
        return pltpu.make_async_remote_copy(
            src_ref=src, dst_ref=dst, send_sem=sems[0], recv_sem=sems[1],
            device_id=peer, device_id_type=pl.DeviceIdType.MESH,
        )

    def pair(sem, *index):
        return sem.at[(0,) + index], sem.at[(1,) + index]

    def columns(i):
        return pl.ds(pl.multiple_of(i * cz, cz), cz)

    barrier = pltpu.get_barrier_semaphore()
    peers = [ypeer, xpeer, cpeer, diag] + [zpeer(d) for d in range(1, planes)]
    own = gat.at[:, z, y, x, c]
    mine = pltpu.make_async_copy(w_ref, own, qloc)
    mine.start()
    for peer in peers:
        pl.semaphore_signal(barrier, inc=1, device_id=peer, device_id_type=pl.DeviceIdType.MESH)
    mine.wait()
    pl.semaphore_wait(barrier, len(peers))

    sends = []

    def go(*copies):
        for one in copies:
            one.start()
            sends.append(one)
        return copies

    def arrived(copies):
        for one in copies:
            one.wait_recv()

    def at(d):
        return lax.rem(z + planes - d, planes)

    zs = [None] + [
        go(copy(own, own, pair(gz, d - 1), zpeer(d)))
        for d in range(1, planes)
    ]

    def spread(d):
        i = at(d)
        a = gat.at[0:2, i, y, x, c]
        b = gat.at[2:4, i, y, x, c]
        links = go(copy(a, a, pair(gay, d), ypeer), copy(b, b, pair(gax, d), xpeer))
        whole = gat.at[:, i, y, x, c]
        return links, go(copy(whole, whole, pair(gc, d, 0), cpeer))

    def spread_again(d):
        i = at(d)
        a = gat.at[0:2, i, :, x, c]
        b = gat.at[2:4, i, y, :, c]
        links = go(copy(a, a, pair(gbx, d), xpeer), copy(b, b, pair(gby, d), ypeer))
        a = gat.at[0:2, i, oy, x, c]
        b = gat.at[2:4, i, y, ox, c]
        return links, go(copy(a, a, pair(gc, d, 1), cpeer), copy(b, b, pair(gc, d, 2), cpeer))

    def share(d):
        i = at(d)
        a = gat.at[0:2, i, :, ox, c]
        b = gat.at[2:4, i, oy, :, c]
        return go(copy(a, a, pair(gc, d, 3), cpeer), copy(b, b, pair(gc, d, 4), cpeer))

    def neighbours(lower, upper, left, right, sem):
        to_right = copy(upper, left, pair(sem, 0), (dp, lax.rem(seq + 1, seqs)))
        to_left = copy(lower, right, pair(sem, 1), (dp, lax.rem(seq + seqs - 1, seqs)))
        return to_right, to_left

    def start_halo(halo):
        pl.when(seq < seqs - 1)(halo[0].start)
        pl.when(seq > 0)(halo[1].start)

    def wait_halo(halo):
        pl.when(seq > 0)(halo[0].wait_recv)
        pl.when(seq < seqs - 1)(halo[1].wait_recv)

    def wait_halo_sends(halo):
        pl.when(seq < seqs - 1)(halo[0].wait_send)
        pl.when(seq > 0)(halo[1].wait_send)

    tile = 32

    def activate_own():
        @pl.loop(0, rows // tile)
        def _(r):
            at_row = pl.multiple_of(r * tile, tile)
            value = in_ref[pl.ds(at_row, tile), :].astype(F32)
            act[pl.ds(pl.multiple_of(gap + at_row, tile), tile), :] = gelu_only(value).astype(BF16)

    def activate_halo():
        for side, start in ((0, 0), (1, gap + rows)):
            inside = (seq > 0) if side == 0 else (seq < seqs - 1)

            @pl.when(inside)
            def _():
                @pl.loop(0, gap // tile)
                def _(r):
                    at_row = pl.multiple_of(r * tile, tile)
                    value = xh[side, pl.ds(at_row, tile), :].astype(F32)
                    act[pl.ds(pl.multiple_of(start + at_row, tile), tile), :] = gelu_only(value).astype(BF16)

            @pl.when(jnp.logical_not(inside))
            def _():
                act[start:start + gap, :] = jnp.zeros((gap, chans), BF16)
                dpre[start:start + gap, :] = jnp.zeros((gap, hidden), BF16)

    def weight(k, i):
        return gat[k, i].reshape(cz, hidden)

    def multiply(d):
        i = at(d)
        for k in range(4):
            left = act[k * gap:k * gap + rows, columns(i)] if k < 3 else cot_ref[:, columns(i)]
            value = jnp.dot(left, weight(k, i), preferred_element_type=F32)
            if d == 0:
                acc[k] = value
            else:
                acc[k] += value

    first, second, cores = {}, {}, {}
    halo = neighbours(in_ref.at[0:gap], in_ref.at[gap:rows], xh.at[0], xh.at[1], hx)
    for t in range(planes + 3):
        if t < planes:
            if t > 0:
                arrived(zs[t])
            first[t], cores[t] = spread(t)
        if t == 0:
            start_halo(halo)
            activate_own()
        if 0 <= t - 1 < planes:
            arrived(first[t - 1])
            second[t - 1], more = spread_again(t - 1)
            cores[t - 1] += more
        if 0 <= t - 2 < planes:
            arrived(second[t - 2])
            cores[t - 2] += share(t - 2)
        if t == 3:
            wait_halo(halo)
            activate_halo()
        if 0 <= t - 3 < planes:
            arrived(cores[t - 3])
            multiply(t - 3)

    @pl.loop(0, rows // tile)
    def _(r):
        here = pl.ds(pl.multiple_of(r * tile, tile), tile)
        pre = acc[0, here, :].astype(BF16).astype(F32)
        pre += acc[1, here, :].astype(BF16).astype(F32)
        pre += acc[2, here, :].astype(BF16).astype(F32)
        value, slope = gelu_and_slope(pre)
        mid[here, :] = value.astype(BF16)
        dpre[pl.ds(pl.multiple_of(gap + r * tile, tile), tile), :] = (acc[3, here, :] * slope).astype(BF16)

    halo_d = neighbours(
        dpre.at[gap:2 * gap], dpre.at[2 * gap:3 * gap],
        dpre.at[0:gap], dpre.at[gap + rows:2 * gap + rows], hd,
    )
    start_halo(halo_d)

    def to(d):
        return lax.rem(z + d, planes)

    def partial(n, d):
        for k in range(4):
            if k < 3:
                left, right = act[k * gap:k * gap + rows, columns(to(d))], dpre[gap:gap + rows, :]
            else:
                left, right = cot_ref[:, columns(to(d))], mid[...]
            value = lax.dot_general(left, right, (((0,), (0,)), ((), ())), preferred_element_type=F32)
            part[n % 2, k] = value.reshape(part.shape[2:])
        sb0[n] = part[n % 2, :, :, :, oc].astype(BF16)
        return go(copy(sb0.at[n], rb0.at[n], pair(q0, n), cpeer))

    def sum_cores(n, copies):
        arrived(copies)
        s0[n % 2] = part[n % 2, :, :, :, c] + rb0[n].astype(F32)
        sb1a[n] = s0[n % 2, 0:2, :, ox].astype(BF16)
        sb1b[n] = s0[n % 2, 2:4, oy].astype(BF16)
        return go(
            copy(sb1a.at[n], rb1a.at[n], pair(q1a, n), xpeer),
            copy(sb1b.at[n], rb1b.at[n], pair(q1b, n), ypeer),
        )

    def sum_first(n, copies):
        arrived(copies)
        s1a[n % 2] = s0[n % 2, 0:2, :, x] + rb1a[n].astype(F32)
        s1b[n % 2] = s0[n % 2, 2:4, y] + rb1b[n].astype(F32)
        sb2a[n] = s1a[n % 2, :, oy].astype(BF16)
        sb2b[n] = s1b[n % 2, :, ox].astype(BF16)
        return go(
            copy(sb2a.at[n], rb2a.at[n], pair(q2a, n), ypeer),
            copy(sb2b.at[n], rb2b.at[n], pair(q2b, n), xpeer),
        )

    def sum_second(n, d, copies):
        arrived(copies)
        s2[0:2] = s1a[n % 2, :, y] + rb2a[n].astype(F32)
        s2[2:4] = s1b[n % 2, :, x] + rb2b[n].astype(F32)
        if d == 0:
            return ()
        sb3[n] = s2[...].astype(BF16)
        return go(copy(sb3.at[n], rb3.at[n], pair(q3, n), zpeer(d)))

    def finish_columns(j):
        here = slice(j * cz, (j + 1) * cz)
        nt = (((1,), (1,)), ((), ()))
        total = lax.dot_general(dpre[2 * gap:4 * gap, :], weight(0, j), nt, preferred_element_type=F32)
        total += lax.dot_general(dpre[gap:3 * gap, :], weight(1, j), nt, preferred_element_type=F32)
        total += lax.dot_general(dpre[0:2 * gap, :], weight(2, j), nt, preferred_element_type=F32)
        dacc[0] = total
        dacc[1] = lax.dot_general(mid[...], weight(3, j), nt, preferred_element_type=F32)

        @pl.loop(0, rows // tile)
        def _(r):
            at_row = pl.ds(pl.multiple_of(r * tile, tile), tile)
            source = in_ref[at_row, here].astype(F32)
            out_ref[at_row, here] = (source + dacc[1, at_row, :]).astype(BF16)
            slope = gelu_and_slope(source)[1]
            ig_ref[at_row, here] = (cot_ref[at_row, here].astype(F32) + dacc[0, at_row, :] * slope).astype(BF16)

    order = list(range(1, planes)) + [0]
    r0, r1, r2, r3 = {}, {}, {}, []
    fills = list(range(planes))
    for t in range(planes + 3):
        if 0 <= t - 3 < planes:
            r3 += sum_second(t - 3, order[t - 3], r2[t - 3])
        if 0 <= t - 2 < planes:
            r2[t - 2] = sum_first(t - 2, r1[t - 2])
        if 0 <= t - 1 < planes:
            r1[t - 1] = sum_cores(t - 1, r0[t - 1])
        if t < planes:
            r0[t] = partial(t, order[t])
        if t >= 2 and fills:
            if t == 2:
                wait_halo(halo_d)
            finish_columns(fills.pop(0))
    for j in fills:
        finish_columns(j)
    arrived(r3)
    total = s2[...]
    for n in range(planes - 1):
        total += rb3[n].astype(F32)
    cg_ref[...] = total * factor

    for one in sends:
        one.wait_send()
    wait_halo_sends(halo)
    wait_halo_sends(halo_d)


def fused(planes, inputs, conv_weight, out_weight, cotangent):
    rows, chans = inputs.shape[1:]
    share, taps, hidden = conv_weight.shape
    factor = 1.0 / math.sqrt(rows * lax.axis_size("seq") * lax.axis_size("dp"))
    w = jnp.concatenate([conv_weight.transpose(1, 0, 2), out_weight[None]], axis=0)
    gap = rows // 2
    dma = pltpu.SemaphoreType.DMA
    blk = (share, hidden)
    cz = chans // planes
    vmem = pltpu.VMEM
    both = lambda shape: [vmem(shape, BF16), vmem(shape, BF16)]
    outputs, input_grad, grads = pl.pallas_call(
        functools.partial(block_kernel, planes, factor),
        out_shape=(
            jax.ShapeDtypeStruct((rows, chans), BF16),
            jax.ShapeDtypeStruct((rows, chans), BF16),
            jax.ShapeDtypeStruct((4,) + blk, F32),
        ),
        in_specs=[pl.BlockSpec(memory_space=pltpu.VMEM)] * 3,
        out_specs=[pl.BlockSpec(memory_space=pltpu.VMEM)] * 3,
        scratch_shapes=[
            vmem((4, planes, 2, 2, 2) + blk, BF16),
            vmem((2, gap, chans), BF16),
            vmem((rows + 2 * gap, chans), BF16),
            vmem((4, rows, hidden), F32),
            vmem((rows, hidden), BF16),
            vmem((rows + 2 * gap, hidden), BF16),
            vmem((2, rows, cz), F32),
            vmem((2, 4, 2, 2, 2) + blk, F32),
            vmem((2, 4, 2, 2) + blk, F32),
            vmem((2, 2, 2) + blk, F32),
            vmem((2, 2, 2) + blk, F32),
            vmem((4,) + blk, F32),
            *both((planes, 4, 2, 2) + blk),
            *both((planes, 2, 2) + blk),
            *both((planes, 2, 2) + blk),
            *both((planes, 2) + blk),
            *both((planes, 2) + blk),
            *both((planes - 1, 4) + blk),
            dma((2, planes - 1)),
            dma((2, planes)),
            dma((2, planes)),
            dma((2, planes)),
            dma((2, planes)),
            dma((2, planes, 5)),
            dma((2, 2)),
            dma((2, 2)),
            dma((2, planes)),
            dma((2, planes)),
            dma((2, planes)),
            dma((2, planes)),
            dma((2, planes)),
            dma((2, planes - 1)),
            dma,
        ],
        compiler_params=pltpu.CompilerParams(
            collective_id=0, has_side_effects=True, vmem_limit_bytes=48 * 1024 * 1024
        ),
        cost_estimate=pl.CostEstimate(
            flops=2 * 12 * rows * chans * hidden, bytes_accessed=8 * rows * chans, transcendentals=0
        ),
    )(inputs[0], cotangent[0], w)
    return outputs[None], input_grad[None], grads[:3].transpose(1, 0, 2), grads[3]


def with_halo(cells, sides, width):
    for axis, dim in sides:
        count = lax.axis_size(axis)
        ends = count - 1
        head = lax.slice_in_dim(cells, 0, width, axis=dim)
        tail = lax.slice_in_dim(cells, cells.shape[dim] - width, cells.shape[dim], axis=dim)
        cells = jnp.concatenate(
            [
                lax.ppermute(tail, axis, [(i, (i + 1) % count) for i in range(ends)]),
                cells,
                lax.ppermute(head, axis, [((i + 1) % count, i) for i in range(ends)]),
            ],
            axis=dim,
        )
    return cells


def by_collectives(inputs, conv_weight, out_weight, cotangent):
    input_rows = inputs.shape[1]
    chans = inputs.shape[2]
    dilation_gap = input_rows // 2
    source = inputs[0]
    upstream = cotangent[0]
    wconv, wout = (
        lax.all_gather(conv_weight, ("dp", "seq"), axis=0, tiled=True),
        lax.all_gather(out_weight, ("dp", "seq"), axis=0, tiled=True),
    )
    hidden = wout.shape[1]
    wflat = wconv.reshape(chans, 3 * hidden)
    activated_value = jax.nn.gelu(source.astype(F32)).astype(BF16)
    widened_input = with_halo(activated_value, (("seq", 0),), dilation_gap)
    pre = jnp.zeros((input_rows, hidden), F32)
    for k in range(3):
        piece = jnp.dot(
            widened_input[k * dilation_gap : k * dilation_gap + input_rows],
            wconv[:, k, :],
            preferred_element_type=F32,
        )
        pre = pre + piece.astype(BF16).astype(F32)
    mid = jax.nn.gelu(pre).astype(BF16)
    outputs = (source.astype(F32) + jnp.dot(mid, wout.T, preferred_element_type=F32)).astype(BF16)
    dmid = jnp.dot(upstream, wout, preferred_element_type=F32)
    dpre = jax.vjp(jax.nn.gelu, pre)[1](dmid)[0].astype(BF16)
    wide = with_halo(dpre, (("seq", 0),), dilation_gap)
    shifted = jnp.concatenate(
        [wide[k * dilation_gap : k * dilation_gap + input_rows] for k in (2, 1, 0)], axis=1
    )
    dact = jnp.dot(shifted, wflat.T, preferred_element_type=F32)
    factor = 1.0 / math.sqrt(input_rows * lax.axis_size("seq") * lax.axis_size("dp"))
    conv_part = (
        jnp.einsum("pc,pk->ck", activated_value, shifted, preferred_element_type=F32) * factor
    ).reshape(chans, 3, hidden)
    out_part = jnp.einsum("pc,ph->ch", upstream, mid, preferred_element_type=F32) * factor
    input_grad = (
        upstream.astype(F32) + jax.vjp(jax.nn.gelu, source.astype(F32))[1](dact)[0]
    ).astype(BF16)
    conv_grad, out_grad = (
        lax.psum_scatter(conv_part, ("dp", "seq"), scatter_dimension=0, tiled=True),
        lax.psum_scatter(out_part, ("dp", "seq"), scatter_dimension=0, tiled=True),
    )
    return (outputs[None], input_grad[None], conv_grad, out_grad)


def solution(mesh):
    planes = mesh.shape["dp"] // 2

    def shards(inputs, conv_weight, out_weight, cotangent):
        aligned = conv_weight.shape[0] % 16 == 0 and mesh.shape["seq"] == 4 and 1 < planes <= 4
        if aligned:
            return fused(planes, inputs, conv_weight, out_weight, cotangent)
        return by_collectives(inputs, conv_weight, out_weight, cotangent)

    return jax.shard_map(
        shards,
        mesh=mesh,
        in_specs=(
            P("dp", "seq", None),
            P(("dp", "seq"), None, None),
            P(("dp", "seq"), None),
            P("dp", "seq", None),
        ),
        out_specs=(
            P("dp", "seq", None),
            P("dp", "seq", None),
            P(("dp", "seq"), None, None),
            P(("dp", "seq"), None),
        ),
        check_vma=False,
    )
```

time: 371 us -> 59.8 us (0.16)
  waiting for transfers between devices: 254 us -> 0 us
  Pallas kernels: 0 us -> 52.7 us
  blocking collectives: 48.5 us -> 0 us
  matrix products: 20.3 us -> 0 us
  local copies, waits for them, and re-layouts: 22 us -> 5.31 us
  between operations: 13.9 us -> 0.65 us
  starting transfers between devices: 9.53 us -> 0 us
    unnamed x5 -> x0, waiting for transfers between devices: 246 us -> none
    pallas_call x0 -> x1, Pallas kernels: none -> 52.7 us  [fused(): pl.pallas_call(functools.partial(block_kernel, planes, factor), out_shape...]
    all_gather x1 -> x0, blocking collectives: 48.5 us -> none  [shards(): lax.all_gather(out_weight, ('dp', 'seq'), axis=0, tiled=True)]
    dot_general x8 -> x0, matrix products: 20.3 us -> none  [the longest x3 5.49 us: shards(): jnp.dot(widened_input[kernel_offset * dilation_gap:kernel_offset * dilati...]
    ppermute x4 -> x0, starting transfers between devices: 9.41 us -> none  [the longest x2 6.84 us: with_halo(): lax.ppermute(tail, axis, [(i, (i + 1) % count) for i in range(ends)])]
    all_gather x1 -> x0, waiting for transfers between devices: 7.37 us -> none  [shards(): lax.all_gather(conv_weight, ('dp', 'seq'), axis=0, tiled=True)]
    reshape x1 -> x0, local copies, waits for them, and re-layouts: 7.16 us -> none  [shards(): conv_part = (jnp.einsum('pc,pk->ck', activated_value, offset_input, prefe...]
    mul x1 -> x0, local copies, waits for them, and re-layouts: 6.04 us -> none  [shards(): jnp.einsum('pc,pk->ck', activated_value, offset_input, preferred_element_...]
  transfers between devices with their start and end apart: 7 -> 0, of which waited for: 4 -> 0; matrix products, arithmetic and copies ran while one was open for 6% -> 0% of each run, Pallas kernels for 0% -> 0%
where the time goes in v1:
time: 59.8 us; the launch traced here: 59.5 us
  Pallas kernels  52.7 us (88%)
  local copies, waits for them, and re-layouts  5.31 us (9%)
  other arithmetic  0.92 us (2%)
  between operations  0.65 us (1%)
    pallas_call x1, Pallas kernels, fused(): pl.pallas_call(functools.partial(block_kernel, planes, factor), out_shape...  52.7 us
    unnamed x6, local copies, waits for them, and re-layouts  4.02 us

profile of v1, /device:TPU:0, one launch (start us, length us, event | category | flops | bytes accessed | tf_op | source)
XLA Modules:
  0.0 59.5 jit_solution(4365527507864397173)
XLA Ops:
  0.6 0.9 %pad_maximum_fusion.w_ref = bf16[4,32,384]{2,1,0:T(8,128)(2,1)S(1)} fusion(bf16[1,32,384]{2,1,0:T(8,128)(2,1)} %bitcast.15, bf16[3,32,384]{2,1,0:T(8,128)(2,1)} %bitcast.14), kind=kLoop, calls=%fused_computation.1 | loop fusion | flops 49152 | bytes 196608 | tf_op jit(solution)/shard_map/concatenate | solution.py:312
  1.6 0.0 copy-start
  1.6 1.1 %copy-done = bf16[1,384,1024]{2,1,0:T(8,128)(2,1)S(1)} copy-done((bf16[1,384,1024]{2,1,0:T(8,128)(2,1)S(1)}, bf16[1,384,1024]{2,1,0:T(8,128)(2,1)}, u32[]{:S(2)}) %copy-start) | copy-done | bytes 786456
  2.7 0.0 copy-start.1
  2.7 1.1 %copy-done.1 = bf16[1,384,1024]{2,1,0:T(8,128)(2,1)S(1)} copy-done((bf16[1,384,1024]{2,1,0:T(8,128)(2,1)S(1)}, bf16[1,384,1024]{2,1,0:T(8,128)(2,1)}, u32[]{:S(2)}) %copy-start.1) | copy-done | bytes 786456
  3.8 52.7 %shard_map.75 = (bf16[384,1024]{1,0:T(8,128)(2,1)S(1)}, bf16[384,1024]{1,0:T(8,128)(2,1)S(1)}, f32[4,32,384]{2,1,0:T(8,128)S(1)}) custom-call(bf16[384,1024]{1,0:T(8,128)(2,1)S(1)} %bitcast.12, bf16[384,1024]{1,0:T(8,128)(2,1)S(1)} %bitcast.13, bf16[4,32,384]{2,1,0:T(8,128)(2,1)S(1)} %pad_maximum_fusion.w_ref), custom_call_target="tpu_custom_call" | custom-call | flops 3623878656 | bytes 3145728 | tf_op jit(solution)/shard_map/pallas_call | solution.py:319
  56.5 0.6 %slice_bitcast_fusion.1 = f32[32,384]{1,0:T(8,128)} fusion(f32[4,32,384]{2,1,0:T(8,128)S(1)} %get-tuple-element.9), kind=kLoop, calls=%fused_computation.2 | loop fusion | bytes 98304 | tf_op jit(solution)/shard_map/squeeze | solution.py:370
  57.1 0.7 %slice_bitcast_fusion = f32[32,3,384]{2,0,1:T(8,128)} fusion(f32[4,32,384]{2,1,0:T(8,128)S(1)} %get-tuple-element.9), kind=kLoop, calls=%fused_computation | loop fusion | bytes 294912 | tf_op jit(solution)/shard_map/transpose | solution.py:370
  57.8 0.9 %copy.10 = bf16[1,384,1024]{2,1,0:T(8,128)(2,1)} copy(bf16[1,384,1024]{2,1,0:T(8,128)(2,1)S(1)} %bitcast.11) | data formatting | bytes 1572864
  58.7 0.9 %copy.11 = bf16[1,384,1024]{2,1,0:T(8,128)(2,1)} copy(bf16[1,384,1024]{2,1,0:T(8,128)(2,1)S(1)} %bitcast.10) | data formatting | bytes 1572864
Async XLA Ops:
  1.6 1.1 %copy-start = (bf16[1,384,1024]{2,1,0:T(8,128)(2,1)S(1)}, bf16[1,384,1024]{2,1,0:T(8,128)(2,1)}, u32[]{:S(2)}) copy-start(bf16[1,384,1024]{2,1,0:T(8,128)(2,1)} %param.4) | copy-start | bytes 2359300
  2.7 1.1 %copy-start.1 = (bf16[1,384,1024]{2,1,0:T(8,128)(2,1)S(1)}, bf16[1,384,1024]{2,1,0:T(8,128)(2,1)}, u32[]{:S(2)}) copy-start(bf16[1,384,1024]{2,1,0:T(8,128)(2,1)} %param.7) | copy-start | bytes 2359300

commit v2 on v1

--- a/solution.py
+++ b/solution.py
@@ -29,11 +29,11 @@
 
 def block_kernel(
     planes, factor,
-    in_ref, cot_ref, w_ref,
+    in_hbm, cot_hbm, w_ref,
     out_ref, ig_ref, cg_ref,
-    gat, xh, act, acc, mid, dpre, dacc, part, s0, s1a, s1b, s2,
+    in_ref, cot_ref, gat, xh, act, acc, mid, dpre, dacc, part, s0, s1a, s1b, s2,
     sb0, rb0, sb1a, rb1a, sb1b, rb1b, sb2a, rb2a, sb2b, rb2b, sb3, rb3,
-    gz, gax, gay, gbx, gby, gc, hx, hd, q0, q1a, q1b, q2a, q2b, q3, qloc,
+    gz, gax, gay, gbx, gby, gc, hx, hd, q0, q1a, q1b, q2a, q2b, q3, qz, qloc,
 ):
     dp = lax.axis_index("dp")
     seq = lax.axis_index("seq")
@@ -50,8 +50,11 @@
     cpeer = (dp, x * 2 + oc)
     diag = (dp, ox * 2 + oc)
 
-    def zpeer(d):
-        return (lax.rem(z + d, planes) * 2 + y, seq)
+    inner = ((z + 1) // 2) % 2
+    flips = (z, z + 1 - 2 * (z % 2), lax.rem(z + 2, planes), planes - 1 - z)
+
+    def zpeer(e):
+        return (flips[e] * 2 + y, seq)
 
     def copy(src, dst, sems, peer):
         return pltpu.make_async_remote_copy(
@@ -68,8 +71,12 @@
     barrier = pltpu.get_barrier_semaphore()
     peers = [ypeer, xpeer, cpeer, diag] + [zpeer(d) for d in range(1, planes)]
     own = gat.at[:, z, y, x, c]
-    mine = pltpu.make_async_copy(w_ref, own, qloc)
+    mine = pltpu.make_async_copy(w_ref, own, qloc.at[0])
+    load_in = pltpu.make_async_copy(in_hbm, in_ref, qloc.at[1])
+    load_cot = pltpu.make_async_copy(cot_hbm, cot_ref, qloc.at[2])
     mine.start()
+    load_in.start()
+    load_cot.start()
     for peer in peers:
         pl.semaphore_signal(barrier, inc=1, device_id=peer, device_id_type=pl.DeviceIdType.MESH)
     mine.wait()
@@ -87,13 +94,34 @@
         for one in copies:
             one.wait_recv()
 
-    def at(d):
-        return lax.rem(z + planes - d, planes)
-
-    zs = [None] + [
-        go(copy(own, own, pair(gz, d - 1), zpeer(d)))
-        for d in range(1, planes)
-    ]
+    def at(n):
+        if n < 2:
+            return flips[n]
+        near, far = (flips[3], flips[2]) if n == 2 else (flips[2], flips[3])
+        return inner * near + (1 - inner) * far
+
+    def plane(n, e, slot, order):
+        piece = gat.at[:, at(n), y, x, c]
+        return pltpu.make_async_remote_copy(
+            src_ref=piece, dst_ref=piece, send_sem=qz.at[slot], recv_sem=gz.at[order - 1],
+            device_id=zpeer(e), device_id_type=pl.DeviceIdType.MESH,
+        )
+
+    next_door = plane(0, 1, 0, 1)
+    across = [plane(0, 3, 1, 2), plane(1, 3, 2, 3), plane(2, 1, 3, 2), plane(3, 1, 4, 3)]
+
+    def landed(n):
+        piece = gat.at[:, at(n), y, x, c]
+        pltpu.make_async_remote_copy(
+            src_ref=piece, dst_ref=piece, send_sem=qz.at[0], recv_sem=gz.at[n - 1],
+            device_id=zpeer(1), device_id_type=pl.DeviceIdType.MESH,
+        ).wait_recv()
+
+    def inside(body):
+        pl.when(inner == 1)(body)
+
+    def outside(body):
+        pl.when(inner == 0)(body)
 
     def spread(d):
         i = at(d)
@@ -146,9 +174,9 @@
 
     def activate_halo():
         for side, start in ((0, 0), (1, gap + rows)):
-            inside = (seq > 0) if side == 0 else (seq < seqs - 1)
-
-            @pl.when(inside)
+            present = (seq > 0) if side == 0 else (seq < seqs - 1)
+
+            @pl.when(present)
             def _():
                 @pl.loop(0, gap // tile)
                 def _(r):
@@ -156,7 +184,7 @@
                     value = xh[side, pl.ds(at_row, tile), :].astype(F32)
                     act[pl.ds(pl.multiple_of(start + at_row, tile), tile), :] = gelu_only(value).astype(BF16)
 
-            @pl.when(jnp.logical_not(inside))
+            @pl.when(jnp.logical_not(present))
             def _():
                 act[start:start + gap, :] = jnp.zeros((gap, chans), BF16)
                 dpre[start:start + gap, :] = jnp.zeros((gap, hidden), BF16)
@@ -176,27 +204,63 @@
 
     first, second, cores = {}, {}, {}
     halo = neighbours(in_ref.at[0:gap], in_ref.at[gap:rows], xh.at[0], xh.at[1], hx)
-    for t in range(planes + 3):
-        if t < planes:
-            if t > 0:
-                arrived(zs[t])
-            first[t], cores[t] = spread(t)
-        if t == 0:
-            start_halo(halo)
-            activate_own()
-        if 0 <= t - 1 < planes:
-            arrived(first[t - 1])
-            second[t - 1], more = spread_again(t - 1)
-            cores[t - 1] += more
-        if 0 <= t - 2 < planes:
-            arrived(second[t - 2])
-            cores[t - 2] += share(t - 2)
-        if t == 3:
-            wait_halo(halo)
-            activate_halo()
-        if 0 <= t - 3 < planes:
-            arrived(cores[t - 3])
-            multiply(t - 3)
+
+    def begin(n):
+        first[n], cores[n] = spread(n)
+
+    def carry_on(n):
+        arrived(first[n])
+        second[n], more = spread_again(n)
+        cores[n] += more
+
+    def hand_over(n):
+        arrived(second[n])
+        cores[n] += share(n)
+
+    def use(n):
+        arrived(cores[n])
+        multiply(n)
+
+    next_door.start()
+    inside(across[0].start)
+    begin(0)
+    load_in.wait()
+    start_halo(halo)
+    activate_own()
+    carry_on(0)
+    landed(1)
+    inside(across[1].start)
+    begin(1)
+
+    @inside
+    def _():
+        landed(2)
+        across[2].start()
+
+    carry_on(1)
+    outside(lambda: landed(2))
+    begin(2)
+
+    @inside
+    def _():
+        landed(3)
+        across[3].start()
+
+    hand_over(0)
+    carry_on(2)
+    wait_halo(halo)
+    activate_halo()
+    load_cot.wait()
+    use(0)
+    outside(lambda: landed(3))
+    begin(3)
+    hand_over(1)
+    use(1)
+    carry_on(3)
+    hand_over(2)
+    use(2)
+    hand_over(3)
+    use(3)
 
     @pl.loop(0, rows // tile)
     def _(r):
@@ -214,8 +278,8 @@
     )
     start_halo(halo_d)
 
-    def to(d):
-        return lax.rem(z + d, planes)
+    def to(e):
+        return flips[e]
 
     def partial(n, d):
         for k in range(4):
@@ -224,15 +288,15 @@
             else:
                 left, right = cot_ref[:, columns(to(d))], mid[...]
             value = lax.dot_general(left, right, (((0,), (0,)), ((), ())), preferred_element_type=F32)
-            part[n % 2, k] = value.reshape(part.shape[2:])
-        sb0[n] = part[n % 2, :, :, :, oc].astype(BF16)
+            part[n, k] = value.reshape(part.shape[2:])
+        sb0[n] = part[n, :, :, :, oc].astype(BF16)
         return go(copy(sb0.at[n], rb0.at[n], pair(q0, n), cpeer))
 
     def sum_cores(n, copies):
         arrived(copies)
-        s0[n % 2] = part[n % 2, :, :, :, c] + rb0[n].astype(F32)
-        sb1a[n] = s0[n % 2, 0:2, :, ox].astype(BF16)
-        sb1b[n] = s0[n % 2, 2:4, oy].astype(BF16)
+        s0[n] = part[n, :, :, :, c] + rb0[n].astype(F32)
+        sb1a[n] = s0[n, 0:2, :, ox].astype(BF16)
+        sb1b[n] = s0[n, 2:4, oy].astype(BF16)
         return go(
             copy(sb1a.at[n], rb1a.at[n], pair(q1a, n), xpeer),
             copy(sb1b.at[n], rb1b.at[n], pair(q1b, n), ypeer),
@@ -240,10 +304,10 @@
 
     def sum_first(n, copies):
         arrived(copies)
-        s1a[n % 2] = s0[n % 2, 0:2, :, x] + rb1a[n].astype(F32)
-        s1b[n % 2] = s0[n % 2, 2:4, y] + rb1b[n].astype(F32)
-        sb2a[n] = s1a[n % 2, :, oy].astype(BF16)
-        sb2b[n] = s1b[n % 2, :, ox].astype(BF16)
+        s1a[n] = s0[n, 0:2, :, x] + rb1a[n].astype(F32)
+        s1b[n] = s0[n, 2:4, y] + rb1b[n].astype(F32)
+        sb2a[n] = s1a[n, :, oy].astype(BF16)
+        sb2b[n] = s1b[n, :, ox].astype(BF16)
         return go(
             copy(sb2a.at[n], rb2a.at[n], pair(q2a, n), ypeer),
             copy(sb2b.at[n], rb2b.at[n], pair(q2b, n), xpeer),
@@ -251,8 +315,8 @@
 
     def sum_second(n, d, copies):
         arrived(copies)
-        s2[0:2] = s1a[n % 2, :, y] + rb2a[n].astype(F32)
-        s2[2:4] = s1b[n % 2, :, x] + rb2b[n].astype(F32)
+        s2[0:2] = s1a[n, :, y] + rb2a[n].astype(F32)
+        s2[2:4] = s1b[n, :, x] + rb2b[n].astype(F32)
         if d == 0:
             return ()
         sb3[n] = s2[...].astype(BF16)
@@ -275,18 +339,18 @@
             slope = gelu_and_slope(source)[1]
             ig_ref[at_row, here] = (cot_ref[at_row, here].astype(F32) + dacc[0, at_row, :] * slope).astype(BF16)
 
-    order = list(range(1, planes)) + [0]
+    order = [2, 3, 1, 0]
     r0, r1, r2, r3 = {}, {}, {}, []
     fills = list(range(planes))
-    for t in range(planes + 3):
-        if 0 <= t - 3 < planes:
-            r3 += sum_second(t - 3, order[t - 3], r2[t - 3])
-        if 0 <= t - 2 < planes:
-            r2[t - 2] = sum_first(t - 2, r1[t - 2])
+    for t in range(planes + 4):
+        if t < planes:
+            r0[t] = partial(t, order[t])
         if 0 <= t - 1 < planes:
             r1[t - 1] = sum_cores(t - 1, r0[t - 1])
-        if t < planes:
-            r0[t] = partial(t, order[t])
+        if 0 <= t - 3 < planes:
+            r2[t - 3] = sum_first(t - 3, r1[t - 3])
+        if 0 <= t - 4 < planes:
+            r3 += sum_second(t - 4, order[t - 4], r2[t - 4])
         if t >= 2 and fills:
             if t == 2:
                 wait_halo(halo_d)
@@ -301,6 +365,13 @@
 
     for one in sends:
         one.wait_send()
+    next_door.wait_send()
+
+    @inside
+    def _():
+        for one in across:
+            one.wait_send()
+
     wait_halo_sends(halo)
     wait_halo_sends(halo_d)
 
@@ -323,9 +394,11 @@
             jax.ShapeDtypeStruct((rows, chans), BF16),
             jax.ShapeDtypeStruct((4,) + blk, F32),
         ),
-        in_specs=[pl.BlockSpec(memory_space=pltpu.VMEM)] * 3,
+        in_specs=[pl.BlockSpec(memory_space=pl.ANY)] * 2 + [pl.BlockSpec(memory_space=pltpu.VMEM)],
         out_specs=[pl.BlockSpec(memory_space=pltpu.VMEM)] * 3,
         scratch_shapes=[
+            vmem((rows, chans), BF16),
+            vmem((rows, chans), BF16),
             vmem((4, planes, 2, 2, 2) + blk, BF16),
             vmem((2, gap, chans), BF16),
             vmem((rows + 2 * gap, chans), BF16),
@@ -333,10 +406,10 @@
             vmem((rows, hidden), BF16),
             vmem((rows + 2 * gap, hidden), BF16),
             vmem((2, rows, cz), F32),
-            vmem((2, 4, 2, 2, 2) + blk, F32),
-            vmem((2, 4, 2, 2) + blk, F32),
-            vmem((2, 2, 2) + blk, F32),
-            vmem((2, 2, 2) + blk, F32),
+            vmem((planes, 4, 2, 2, 2) + blk, F32),
+            vmem((planes, 4, 2, 2) + blk, F32),
+            vmem((planes, 2, 2) + blk, F32),
+            vmem((planes, 2, 2) + blk, F32),
             vmem((4,) + blk, F32),
             *both((planes, 4, 2, 2) + blk),
             *both((planes, 2, 2) + blk),
@@ -344,7 +417,7 @@
             *both((planes, 2) + blk),
             *both((planes, 2) + blk),
             *both((planes - 1, 4) + blk),
-            dma((2, planes - 1)),
+            dma((planes - 1,)),
             dma((2, planes)),
             dma((2, planes)),
             dma((2, planes)),
@@ -358,7 +431,8 @@
             dma((2, planes)),
             dma((2, planes)),
             dma((2, planes - 1)),
-            dma,
+            dma((5,)),
+            dma((3,)),
         ],
         compiler_params=pltpu.CompilerParams(
             collective_id=0, has_side_effects=True, vmem_limit_bytes=48 * 1024 * 1024
@@ -437,7 +511,7 @@
     planes = mesh.shape["dp"] // 2
 
     def shards(inputs, conv_weight, out_weight, cotangent):
-        aligned = conv_weight.shape[0] % 16 == 0 and mesh.shape["seq"] == 4 and 1 < planes <= 4
+        aligned = conv_weight.shape[0] % 16 == 0 and mesh.shape["seq"] == 4 and planes == 4
         if aligned:
             return fused(planes, inputs, conv_weight, out_weight, cotangent)
         return by_collectives(inputs, conv_weight, out_weight, cotangent)

time: 59.8 us -> 60.8 us (1.017)
  Pallas kernels: 52.7 us -> 53.7 us
    pallas_call x1, Pallas kernels: 52.7 us -> 53.7 us  [fused(): pl.pallas_call(functools.partial(block_kernel, planes, factor), out_shape...]
where the time goes in v2:
time: 60.8 us; the launch traced here: 60.6 us
  Pallas kernels  53.7 us (88%)
  local copies, waits for them, and re-layouts  5.31 us (9%)
  other arithmetic  0.92 us (2%)
  between operations  0.65 us (1%)
    pallas_call x1, Pallas kernels, fused(): pl.pallas_call(functools.partial(block_kernel, planes, factor), out_shape...  53.7 us
    unnamed x6, local copies, waits for them, and re-layouts  4.02 us

profile of v2, /device:TPU:0, one launch (start us, length us, event | category | flops | bytes accessed | tf_op | source)
XLA Modules:
  0.0 60.6 jit_solution(10680564340528251860)
XLA Ops:
  0.6 0.9 %pad_maximum_fusion.w_ref = bf16[4,32,384]{2,1,0:T(8,128)(2,1)S(1)} fusion(bf16[1,32,384]{2,1,0:T(8,128)(2,1)} %bitcast.15, bf16[3,32,384]{2,1,0:T(8,128)(2,1)} %bitcast.14), kind=kLoop, calls=%fused_computation.1 | loop fusion | flops 49152 | bytes 196608 | tf_op jit(solution)/shard_map/concatenate | solution.py:383
  1.6 0.0 copy-start
  1.6 1.1 %copy-done = bf16[1,384,1024]{2,1,0:T(8,128)(2,1)S(1)} copy-done((bf16[1,384,1024]{2,1,0:T(8,128)(2,1)S(1)}, bf16[1,384,1024]{2,1,0:T(8,128)(2,1)}, u32[]{:S(2)}) %copy-start) | copy-done | bytes 786456
  2.7 0.0 copy-start.1
  2.7 1.1 %copy-done.1 = bf16[1,384,1024]{2,1,0:T(8,128)(2,1)S(1)} copy-done((bf16[1,384,1024]{2,1,0:T(8,128)(2,1)S(1)}, bf16[1,384,1024]{2,1,0:T(8,128)(2,1)}, u32[]{:S(2)}) %copy-start.1) | copy-done | bytes 786456
  3.8 53.7 %shard_map.75 = (bf16[384,1024]{1,0:T(8,128)(2,1)S(1)}, bf16[384,1024]{1,0:T(8,128)(2,1)S(1)}, f32[4,32,384]{2,1,0:T(8,128)S(1)}) custom-call(bf16[384,1024]{1,0:T(8,128)(2,1)S(1)} %bitcast.12, bf16[384,1024]{1,0:T(8,128)(2,1)S(1)} %bitcast.13, bf16[4,32,384]{2,1,0:T(8,128)(2,1)S(1)} %pad_maximum_fusion.w_ref), custom_call_target="tpu_custom_call" | custom-call | flops 3623878656 | bytes 3145728 | tf_op jit(solution)/shard_map/pallas_call | solution.py:390
  57.5 0.6 %slice_bitcast_fusion.1 = f32[32,384]{1,0:T(8,128)} fusion(f32[4,32,384]{2,1,0:T(8,128)S(1)} %get-tuple-element.9), kind=kLoop, calls=%fused_computation.2 | loop fusion | bytes 98304 | tf_op jit(solution)/shard_map/squeeze | solution.py:444
  58.2 0.7 %slice_bitcast_fusion = f32[32,3,384]{2,0,1:T(8,128)} fusion(f32[4,32,384]{2,1,0:T(8,128)S(1)} %get-tuple-element.9), kind=kLoop, calls=%fused_computation | loop fusion | bytes 294912 | tf_op jit(solution)/shard_map/transpose | solution.py:444
  58.8 0.9 %copy.10 = bf16[1,384,1024]{2,1,0:T(8,128)(2,1)} copy(bf16[1,384,1024]{2,1,0:T(8,128)(2,1)S(1)} %bitcast.11) | data formatting | bytes 1572864
  59.7 0.9 %copy.11 = bf16[1,384,1024]{2,1,0:T(8,128)(2,1)} copy(bf16[1,384,1024]{2,1,0:T(8,128)(2,1)S(1)} %bitcast.10) | data formatting | bytes 1572864
Async XLA Ops:
  1.6 1.1 %copy-start = (bf16[1,384,1024]{2,1,0:T(8,128)(2,1)S(1)}, bf16[1,384,1024]{2,1,0:T(8,128)(2,1)}, u32[]{:S(2)}) copy-start(bf16[1,384,1024]{2,1,0:T(8,128)(2,1)} %param.4) | copy-start | bytes 2359300
  2.7 1.1 %copy-start.1 = (bf16[1,384,1024]{2,1,0:T(8,128)(2,1)S(1)}, bf16[1,384,1024]{2,1,0:T(8,128)(2,1)}, u32[]{:S(2)}) copy-start(bf16[1,384,1024]{2,1,0:T(8,128)(2,1)} %param.7) | copy-start | bytes 2359300

commit v3 on v2

--- a/solution.py
+++ b/solution.py
@@ -30,10 +30,10 @@
 def block_kernel(
     planes, factor,
     in_hbm, cot_hbm, w_ref,
-    out_ref, ig_ref, cg_ref,
-    in_ref, cot_ref, gat, xh, act, acc, mid, dpre, dacc, part, s0, s1a, s1b, s2,
+    out_hbm, ig_hbm, cg_ref,
+    in_ref, cot_ref, out_ref, ig_ref, gat, xh, act, acc, mid, dpre, dacc, part, s0, s1a, s1b, s2,
     sb0, rb0, sb1a, rb1a, sb1b, rb1b, sb2a, rb2a, sb2b, rb2b, sb3, rb3,
-    gz, gax, gay, gbx, gby, gc, hx, hd, q0, q1a, q1b, q2a, q2b, q3, qz, qloc,
+    gz, gax, gay, gbx, gby, gc, hx, hd, q0, q1a, q1b, q2a, q2b, q3, qz, qloc, qout,
 ):
     dp = lax.axis_index("dp")
     seq = lax.axis_index("seq")
@@ -50,7 +50,6 @@
     cpeer = (dp, x * 2 + oc)
     diag = (dp, ox * 2 + oc)
 
-    inner = ((z + 1) // 2) % 2
     flips = (z, z + 1 - 2 * (z % 2), lax.rem(z + 2, planes), planes - 1 - z)
 
     def zpeer(e):
@@ -95,56 +94,47 @@
             one.wait_recv()
 
     def at(n):
-        if n < 2:
-            return flips[n]
-        near, far = (flips[3], flips[2]) if n == 2 else (flips[2], flips[3])
-        return inner * near + (1 - inner) * far
-
-    def plane(n, e, slot, order):
-        piece = gat.at[:, at(n), y, x, c]
-        return pltpu.make_async_remote_copy(
-            src_ref=piece, dst_ref=piece, send_sem=qz.at[slot], recv_sem=gz.at[order - 1],
-            device_id=zpeer(e), device_id_type=pl.DeviceIdType.MESH,
-        )
-
-    next_door = plane(0, 1, 0, 1)
-    across = [plane(0, 3, 1, 2), plane(1, 3, 2, 3), plane(2, 1, 3, 2), plane(3, 1, 4, 3)]
-
-    def landed(n):
-        piece = gat.at[:, at(n), y, x, c]
-        pltpu.make_async_remote_copy(
-            src_ref=piece, dst_ref=piece, send_sem=qz.at[0], recv_sem=gz.at[n - 1],
-            device_id=zpeer(1), device_id_type=pl.DeviceIdType.MESH,
-        ).wait_recv()
-
-    def inside(body):
-        pl.when(inner == 1)(body)
-
-    def outside(body):
-        pl.when(inner == 0)(body)
-
-    def spread(d):
-        i = at(d)
+        return flips[n]
+
+    def taps(n):
+        return 4 if n == 0 else 3
+
+    def spread(n):
+        i = at(n)
         a = gat.at[0:2, i, y, x, c]
-        b = gat.at[2:4, i, y, x, c]
-        links = go(copy(a, a, pair(gay, d), ypeer), copy(b, b, pair(gax, d), xpeer))
-        whole = gat.at[:, i, y, x, c]
-        return links, go(copy(whole, whole, pair(gc, d, 0), cpeer))
-
-    def spread_again(d):
-        i = at(d)
+        b = gat.at[2:taps(n), i, y, x, c]
+        links = go(copy(a, a, pair(gay, n), ypeer), copy(b, b, pair(gax, n), xpeer))
+        whole = gat.at[0:taps(n), i, y, x, c]
+        return links, go(copy(whole, whole, pair(gc, n, 0), cpeer))
+
+    def spread_again(n):
+        i = at(n)
         a = gat.at[0:2, i, :, x, c]
-        b = gat.at[2:4, i, y, :, c]
-        links = go(copy(a, a, pair(gbx, d), xpeer), copy(b, b, pair(gby, d), ypeer))
+        b = gat.at[2:taps(n), i, y, :, c]
+        links = go(copy(a, a, pair(gbx, n), xpeer), copy(b, b, pair(gby, n), ypeer))
         a = gat.at[0:2, i, oy, x, c]
-        b = gat.at[2:4, i, y, ox, c]
-        return links, go(copy(a, a, pair(gc, d, 1), cpeer), copy(b, b, pair(gc, d, 2), cpeer))
-
-    def share(d):
-        i = at(d)
+        b = gat.at[2:taps(n), i, y, ox, c]
+        return links, go(copy(a, a, pair(gc, n, 1), cpeer), copy(b, b, pair(gc, n, 2), cpeer))
+
+    def share(n):
+        i = at(n)
         a = gat.at[0:2, i, :, ox, c]
-        b = gat.at[2:4, i, oy, :, c]
-        return go(copy(a, a, pair(gc, d, 3), cpeer), copy(b, b, pair(gc, d, 4), cpeer))
+        b = gat.at[2:taps(n), i, oy, :, c]
+        return go(copy(a, a, pair(gc, n, 3), cpeer), copy(b, b, pair(gc, n, 4), cpeer))
+
+    own_taps = gat.at[0:3, z, y, x, c]
+    zs = [()] + [
+        go(copy(own_taps, own_taps, pair(gz, n - 1), zpeer(n))) for n in range(1, planes)
+    ]
+
+    def send_projection():
+        a = gat.at[3, z, :, :, c]
+        return [()] + [go(copy(a, a, pair(qz, n - 1), zpeer(n))) for n in range(1, planes)]
+
+    def share_projection(n, copies):
+        arrived(copies)
+        a = gat.at[3, at(n), :, :, c]
+        return go(copy(a, a, pair(gc, n, 5), cpeer))
 
     def neighbours(lower, upper, left, right, sem):
         to_right = copy(upper, left, pair(sem, 0), (dp, lax.rem(seq + 1, seqs)))
@@ -192,12 +182,12 @@
     def weight(k, i):
         return gat[k, i].reshape(cz, hidden)
 
-    def multiply(d):
-        i = at(d)
-        for k in range(4):
+    def multiply(n, some):
+        i = at(n)
+        for k in some:
             left = act[k * gap:k * gap + rows, columns(i)] if k < 3 else cot_ref[:, columns(i)]
             value = jnp.dot(left, weight(k, i), preferred_element_type=F32)
-            if d == 0:
+            if n == 0:
                 acc[k] = value
             else:
                 acc[k] += value
@@ -219,48 +209,34 @@
 
     def use(n):
         arrived(cores[n])
-        multiply(n)
-
-    next_door.start()
-    inside(across[0].start)
+        multiply(n, range(taps(n)))
+
     begin(0)
     load_in.wait()
     start_halo(halo)
     activate_own()
     carry_on(0)
-    landed(1)
-    inside(across[1].start)
-    begin(1)
-
-    @inside
-    def _():
-        landed(2)
-        across[2].start()
-
-    carry_on(1)
-    outside(lambda: landed(2))
-    begin(2)
-
-    @inside
-    def _():
-        landed(3)
-        across[3].start()
-
     hand_over(0)
-    carry_on(2)
+    projection = send_projection()
+    for n in range(1, planes):
+        arrived(zs[n])
+        begin(n)
+        if n > 1:
+            carry_on(n - 1)
     wait_halo(halo)
     activate_halo()
+    hand_over(1)
+    carry_on(planes - 1)
     load_cot.wait()
     use(0)
-    outside(lambda: landed(3))
-    begin(3)
-    hand_over(1)
     use(1)
-    carry_on(3)
-    hand_over(2)
-    use(2)
-    hand_over(3)
-    use(3)
+    for n in range(2, planes):
+        hand_over(n)
+        use(n)
+    rest = [share_projection(n, projection[n]) for n in range(1, planes)]
+    for n in range(1, planes):
+        arrived(rest[n - 1])
+        multiply(n, (3,))
 
     @pl.loop(0, rows // tile)
     def _(r):
@@ -338,6 +314,15 @@
             out_ref[at_row, here] = (source + dacc[1, at_row, :]).astype(BF16)
             slope = gelu_and_slope(source)[1]
             ig_ref[at_row, here] = (cot_ref[at_row, here].astype(F32) + dacc[0, at_row, :] * slope).astype(BF16)
+
+    leaving = []
+
+    def leave(j):
+        here = pl.ds(j * cz, cz)
+        for n, (ref, hbm) in enumerate(((out_ref, out_hbm), (ig_ref, ig_hbm))):
+            one = pltpu.make_async_copy(ref.at[:, here], hbm.at[:, here], qout.at[n, j])
+            one.start()
+            leaving.append(one)
 
     order = [2, 3, 1, 0]
     r0, r1, r2, r3 = {}, {}, {}, []
@@ -354,9 +339,11 @@
         if t >= 2 and fills:
             if t == 2:
                 wait_halo(halo_d)
-            finish_columns(fills.pop(0))
+            finish_columns(fills[0])
+            leave(fills.pop(0))
     for j in fills:
         finish_columns(j)
+        leave(j)
     arrived(r3)
     total = s2[...]
     for n in range(planes - 1):
@@ -365,13 +352,8 @@
 
     for one in sends:
         one.wait_send()
-    next_door.wait_send()
-
-    @inside
-    def _():
-        for one in across:
-            one.wait_send()
-
+    for one in leaving:
+        one.wait()
     wait_halo_sends(halo)
     wait_halo_sends(halo_d)
 
@@ -395,8 +377,10 @@
             jax.ShapeDtypeStruct((4,) + blk, F32),
         ),
         in_specs=[pl.BlockSpec(memory_space=pl.ANY)] * 2 + [pl.BlockSpec(memory_space=pltpu.VMEM)],
-        out_specs=[pl.BlockSpec(memory_space=pltpu.VMEM)] * 3,
+        out_specs=[pl.BlockSpec(memory_space=pl.ANY)] * 2 + [pl.BlockSpec(memory_space=pltpu.VMEM)],
         scratch_shapes=[
+            vmem((rows, chans), BF16),
+            vmem((rows, chans), BF16),
             vmem((rows, chans), BF16),
             vmem((rows, chans), BF16),
             vmem((4, planes, 2, 2, 2) + blk, BF16),
@@ -417,12 +401,12 @@
             *both((planes, 2) + blk),
             *both((planes, 2) + blk),
             *both((planes - 1, 4) + blk),
-            dma((planes - 1,)),
-            dma((2, planes)),
-            dma((2, planes)),
-            dma((2, planes)),
-            dma((2, planes)),
-            dma((2, planes, 5)),
+            dma((2, planes - 1)),
+            dma((2, planes)),
+            dma((2, planes)),
+            dma((2, planes)),
+            dma((2, planes)),
+            dma((2, planes, 6)),
             dma((2, 2)),
             dma((2, 2)),
             dma((2, planes)),
@@ -431,8 +415,9 @@
             dma((2, planes)),
             dma((2, planes)),
             dma((2, planes - 1)),
-            dma((5,)),
+            dma((2, planes - 1)),
             dma((3,)),
+            dma((2, planes)),
         ],
         compiler_params=pltpu.CompilerParams(
             collective_id=0, has_side_effects=True, vmem_limit_bytes=48 * 1024 * 1024

time: 60.8 us -> 61.3 us (level)
  no operation moved by 1% of the time
where the time goes in v3:
time: 61.3 us; the launch traced here: 61 us
  Pallas kernels  54.1 us (88%)
  local copies, waits for them, and re-layouts  5.31 us (9%)
  other arithmetic  0.92 us (2%)
  between operations  0.65 us (1%)
    pallas_call x1, Pallas kernels, fused(): pl.pallas_call(functools.partial(block_kernel, planes, factor), out_shape...  54.1 us
    unnamed x6, local copies, waits for them, and re-layouts  4.02 us

profile of v3, /device:TPU:0, one launch (start us, length us, event | category | flops | bytes accessed | tf_op | source)
XLA Modules:
  0.0 61.0 jit_solution(14226238964947877036)
XLA Ops:
  0.6 0.9 %pad_maximum_fusion.w_ref = bf16[4,32,384]{2,1,0:T(8,128)(2,1)S(1)} fusion(bf16[1,32,384]{2,1,0:T(8,128)(2,1)} %bitcast.15, bf16[3,32,384]{2,1,0:T(8,128)(2,1)} %bitcast.14), kind=kLoop, calls=%fused_computation.1 | loop fusion | flops 49152 | bytes 196608 | tf_op jit(solution)/shard_map/concatenate | solution.py:365
  1.6 0.0 copy-start
  1.6 1.1 %copy-done = bf16[1,384,1024]{2,1,0:T(8,128)(2,1)S(1)} copy-done((bf16[1,384,1024]{2,1,0:T(8,128)(2,1)S(1)}, bf16[1,384,1024]{2,1,0:T(8,128)(2,1)}, u32[]{:S(2)}) %copy-start) | copy-done | bytes 786456
  2.7 0.0 copy-start.1
  2.7 1.1 %copy-done.1 = bf16[1,384,1024]{2,1,0:T(8,128)(2,1)S(1)} copy-done((bf16[1,384,1024]{2,1,0:T(8,128)(2,1)S(1)}, bf16[1,384,1024]{2,1,0:T(8,128)(2,1)}, u32[]{:S(2)}) %copy-start.1) | copy-done | bytes 786456
  3.8 54.1 %shard_map.75 = (bf16[384,1024]{1,0:T(8,128)(2,1)S(1)}, bf16[384,1024]{1,0:T(8,128)(2,1)S(1)}, f32[4,32,384]{2,1,0:T(8,128)S(1)}) custom-call(bf16[384,1024]{1,0:T(8,128)(2,1)S(1)} %bitcast.12, bf16[384,1024]{1,0:T(8,128)(2,1)S(1)} %bitcast.13, bf16[4,32,384]{2,1,0:T(8,128)(2,1)S(1)} %pad_maximum_fusion.w_ref), custom_call_target="tpu_custom_call" | custom-call | flops 3623878656 | bytes 3145728 | tf_op jit(solution)/shard_map/pallas_call | solution.py:372
  58.0 0.6 %slice_bitcast_fusion.1 = f32[32,384]{1,0:T(8,128)} fusion(f32[4,32,384]{2,1,0:T(8,128)S(1)} %get-tuple-element.9), kind=kLoop, calls=%fused_computation.2 | loop fusion | bytes 98304 | tf_op jit(solution)/shard_map/squeeze | solution.py:429
  58.6 0.7 %slice_bitcast_fusion = f32[32,3,384]{2,0,1:T(8,128)} fusion(f32[4,32,384]{2,1,0:T(8,128)S(1)} %get-tuple-element.9), kind=kLoop, calls=%fused_computation | loop fusion | bytes 294912 | tf_op jit(solution)/shard_map/transpose | solution.py:429
  59.3 0.9 %copy.10 = bf16[1,384,1024]{2,1,0:T(8,128)(2,1)} copy(bf16[1,384,1024]{2,1,0:T(8,128)(2,1)S(1)} %bitcast.11) | data formatting | bytes 1572864
  60.2 0.9 %copy.11 = bf16[1,384,1024]{2,1,0:T(8,128)(2,1)} copy(bf16[1,384,1024]{2,1,0:T(8,128)(2,1)S(1)} %bitcast.10) | data formatting | bytes 1572864
Async XLA Ops:
  1.6 1.1 %copy-start = (bf16[1,384,1024]{2,1,0:T(8,128)(2,1)S(1)}, bf16[1,384,1024]{2,1,0:T(8,128)(2,1)}, u32[]{:S(2)}) copy-start(bf16[1,384,1024]{2,1,0:T(8,128)(2,1)} %param.4) | copy-start | bytes 2359300
  2.7 1.1 %copy-start.1 = (bf16[1,384,1024]{2,1,0:T(8,128)(2,1)S(1)}, bf16[1,384,1024]{2,1,0:T(8,128)(2,1)}, u32[]{:S(2)}) copy-start(bf16[1,384,1024]{2,1,0:T(8,128)(2,1)} %param.7) | copy-start | bytes 2359300

commit v4 on v1

--- a/solution.py
+++ b/solution.py
@@ -29,9 +29,9 @@
 
 def block_kernel(
     planes, factor,
-    in_ref, cot_ref, w_ref,
+    in_hbm, cot_hbm, w_ref,
     out_ref, ig_ref, cg_ref,
-    gat, xh, act, acc, mid, dpre, dacc, part, s0, s1a, s1b, s2,
+    in_ref, cot_ref, gat, xh, act, acc, mid, dpre, dacc, part, s0, s1a, s1b, s2,
     sb0, rb0, sb1a, rb1a, sb1b, rb1b, sb2a, rb2a, sb2b, rb2b, sb3, rb3,
     gz, gax, gay, gbx, gby, gc, hx, hd, q0, q1a, q1b, q2a, q2b, q3, qloc,
 ):
@@ -68,8 +68,12 @@
     barrier = pltpu.get_barrier_semaphore()
     peers = [ypeer, xpeer, cpeer, diag] + [zpeer(d) for d in range(1, planes)]
     own = gat.at[:, z, y, x, c]
-    mine = pltpu.make_async_copy(w_ref, own, qloc)
+    mine = pltpu.make_async_copy(w_ref, own, qloc.at[0])
+    load_in = pltpu.make_async_copy(in_hbm, in_ref, qloc.at[1])
+    load_cot = pltpu.make_async_copy(cot_hbm, cot_ref, qloc.at[2])
     mine.start()
+    load_in.start()
+    load_cot.start()
     for peer in peers:
         pl.semaphore_signal(barrier, inc=1, device_id=peer, device_id_type=pl.DeviceIdType.MESH)
     mine.wait()
@@ -182,6 +186,7 @@
                 arrived(zs[t])
             first[t], cores[t] = spread(t)
         if t == 0:
+            load_in.wait()
             start_halo(halo)
             activate_own()
         if 0 <= t - 1 < planes:
@@ -194,6 +199,7 @@
         if t == 3:
             wait_halo(halo)
             activate_halo()
+            load_cot.wait()
         if 0 <= t - 3 < planes:
             arrived(cores[t - 3])
             multiply(t - 3)
@@ -224,15 +230,15 @@
             else:
                 left, right = cot_ref[:, columns(to(d))], mid[...]
             value = lax.dot_general(left, right, (((0,), (0,)), ((), ())), preferred_element_type=F32)
-            part[n % 2, k] = value.reshape(part.shape[2:])
-        sb0[n] = part[n % 2, :, :, :, oc].astype(BF16)
+            part[n, k] = value.reshape(part.shape[2:])
+        sb0[n] = part[n, :, :, :, oc].astype(BF16)
         return go(copy(sb0.at[n], rb0.at[n], pair(q0, n), cpeer))
 
     def sum_cores(n, copies):
         arrived(copies)
-        s0[n % 2] = part[n % 2, :, :, :, c] + rb0[n].astype(F32)
-        sb1a[n] = s0[n % 2, 0:2, :, ox].astype(BF16)
-        sb1b[n] = s0[n % 2, 2:4, oy].astype(BF16)
+        s0[n] = part[n, :, :, :, c] + rb0[n].astype(F32)
+        sb1a[n] = s0[n, 0:2, :, ox].astype(BF16)
+        sb1b[n] = s0[n, 2:4, oy].astype(BF16)
         return go(
             copy(sb1a.at[n], rb1a.at[n], pair(q1a, n), xpeer),
             copy(sb1b.at[n], rb1b.at[n], pair(q1b, n), ypeer),
@@ -240,10 +246,10 @@
 
     def sum_first(n, copies):
         arrived(copies)
-        s1a[n % 2] = s0[n % 2, 0:2, :, x] + rb1a[n].astype(F32)
-        s1b[n % 2] = s0[n % 2, 2:4, y] + rb1b[n].astype(F32)
-        sb2a[n] = s1a[n % 2, :, oy].astype(BF16)
-        sb2b[n] = s1b[n % 2, :, ox].astype(BF16)
+        s1a[n] = s0[n, 0:2, :, x] + rb1a[n].astype(F32)
+        s1b[n] = s0[n, 2:4, y] + rb1b[n].astype(F32)
+        sb2a[n] = s1a[n, :, oy].astype(BF16)
+        sb2b[n] = s1b[n, :, ox].astype(BF16)
         return go(
             copy(sb2a.at[n], rb2a.at[n], pair(q2a, n), ypeer),
             copy(sb2b.at[n], rb2b.at[n], pair(q2b, n), xpeer),
@@ -251,8 +257,8 @@
 
     def sum_second(n, d, copies):
         arrived(copies)
-        s2[0:2] = s1a[n % 2, :, y] + rb2a[n].astype(F32)
-        s2[2:4] = s1b[n % 2, :, x] + rb2b[n].astype(F32)
+        s2[0:2] = s1a[n, :, y] + rb2a[n].astype(F32)
+        s2[2:4] = s1b[n, :, x] + rb2b[n].astype(F32)
         if d == 0:
             return ()
         sb3[n] = s2[...].astype(BF16)
@@ -278,15 +284,15 @@
     order = list(range(1, planes)) + [0]
     r0, r1, r2, r3 = {}, {}, {}, []
     fills = list(range(planes))
-    for t in range(planes + 3):
-        if 0 <= t - 3 < planes:
-            r3 += sum_second(t - 3, order[t - 3], r2[t - 3])
-        if 0 <= t - 2 < planes:
-            r2[t - 2] = sum_first(t - 2, r1[t - 2])
+    for t in range(planes + 4):
+        if t < planes:
+            r0[t] = partial(t, order[t])
         if 0 <= t - 1 < planes:
             r1[t - 1] = sum_cores(t - 1, r0[t - 1])
-        if t < planes:
-            r0[t] = partial(t, order[t])
+        if 0 <= t - 3 < planes:
+            r2[t - 3] = sum_first(t - 3, r1[t - 3])
+        if 0 <= t - 4 < planes:
+            r3 += sum_second(t - 4, order[t - 4], r2[t - 4])
         if t >= 2 and fills:
             if t == 2:
                 wait_halo(halo_d)
@@ -323,9 +329,11 @@
             jax.ShapeDtypeStruct((rows, chans), BF16),
             jax.ShapeDtypeStruct((4,) + blk, F32),
         ),
-        in_specs=[pl.BlockSpec(memory_space=pltpu.VMEM)] * 3,
+        in_specs=[pl.BlockSpec(memory_space=pltpu.HBM)] * 2 + [pl.BlockSpec(memory_space=pltpu.VMEM)],
         out_specs=[pl.BlockSpec(memory_space=pltpu.VMEM)] * 3,
         scratch_shapes=[
+            vmem((rows, chans), BF16),
+            vmem((rows, chans), BF16),
             vmem((4, planes, 2, 2, 2) + blk, BF16),
             vmem((2, gap, chans), BF16),
             vmem((rows + 2 * gap, chans), BF16),
@@ -333,10 +341,10 @@
             vmem((rows, hidden), BF16),
             vmem((rows + 2 * gap, hidden), BF16),
             vmem((2, rows, cz), F32),
-            vmem((2, 4, 2, 2, 2) + blk, F32),
-            vmem((2, 4, 2, 2) + blk, F32),
-            vmem((2, 2, 2) + blk, F32),
-            vmem((2, 2, 2) + blk, F32),
+            vmem((planes, 4, 2, 2, 2) + blk, F32),
+            vmem((planes, 4, 2, 2) + blk, F32),
+            vmem((planes, 2, 2) + blk, F32),
+            vmem((planes, 2, 2) + blk, F32),
             vmem((4,) + blk, F32),
             *both((planes, 4, 2, 2) + blk),
             *both((planes, 2, 2) + blk),
@@ -358,10 +366,10 @@
             dma((2, planes)),
             dma((2, planes)),
             dma((2, planes - 1)),
-            dma,
+            dma((3,)),
         ],
         compiler_params=pltpu.CompilerParams(
-            collective_id=0, has_side_effects=True, vmem_limit_bytes=48 * 1024 * 1024
+            collective_id=0, has_side_effects=True, vmem_limit_bytes=56 * 1024 * 1024
         ),
         cost_estimate=pl.CostEstimate(
             flops=2 * 12 * rows * chans * hidden, bytes_accessed=8 * rows * chans, transcendentals=0

time: 59.8 us -> 61.7 us (1.032)
  local copies, waits for them, and re-layouts: 5.31 us -> 6.02 us
  other arithmetic: 0.92 us -> 1.56 us
    unnamed x6 -> x4, local copies, waits for them, and re-layouts: 4.02 us -> 3.02 us
    transpose x1, local copies, waits for them, and re-layouts: 0.67 us -> 1.58 us  [fused(): grads[:3].transpose(1, 0, 2)]
    squeeze x1, local copies, waits for them, and re-layouts: 0.62 us -> 1.42 us  [fused(): grads[3]]
    concatenate x1, other arithmetic: 0.92 us -> 1.56 us  [fused(): jnp.concatenate([conv_weight.transpose(1, 0, 2), out_weight[None]], axis=0)]
where the time goes in v4:
time: 61.7 us; the launch traced here: 61.4 us
  Pallas kernels  53.2 us (86%)
  local copies, waits for them, and re-layouts  6.02 us (10%)
  other arithmetic  1.56 us (3%)
  between operations  0.64 us (1%)
    pallas_call x1, Pallas kernels, fused(): pl.pallas_call(functools.partial(block_kernel, planes, factor), out_shape...  53.2 us
    unnamed x4, local copies, waits for them, and re-layouts  3.02 us
    transpose x1, local copies, waits for them, and re-layouts, fused(): grads[:3].transpose(1, 0, 2)  1.58 us
    concatenate x1, other arithmetic, fused(): jnp.concatenate([conv_weight.transpose(1, 0, 2), out_weight[None]], axis=0)  1.56 us
    squeeze x1, local copies, waits for them, and re-layouts, fused(): grads[3]  1.42 us

profile of v4, /device:TPU:0, one launch (start us, length us, event | category | flops | bytes accessed | tf_op | source)
XLA Modules:
  0.0 61.4 jit_solution(4262927038191489041)
XLA Ops:
  0.6 1.6 %pad_maximum_fusion.w_ref = bf16[4,32,384]{2,1,0:T(8,128)(2,1)} fusion(bf16[1,32,384]{2,1,0:T(8,128)(2,1)} %bitcast.13, bf16[3,32,384]{2,1,0:T(8,128)(2,1)} %bitcast.12), kind=kLoop, calls=%fused_computation.1 | loop fusion | flops 49152 | bytes 196608 | tf_op jit(solution)/shard_map/concatenate | solution.py:318
  2.2 53.2 %shard_map.75 = (bf16[384,1024]{1,0:T(8,128)(2,1)}, bf16[384,1024]{1,0:T(8,128)(2,1)}, f32[4,32,384]{2,1,0:T(8,128)}) custom-call(bf16[384,1024]{1,0:T(8,128)(2,1)} %bitcast.14, bf16[384,1024]{1,0:T(8,128)(2,1)} %bitcast.15, bf16[4,32,384]{2,1,0:T(8,128)(2,1)} %pad_maximum_fusion.w_ref), custom_call_target="tpu_custom_call" | custom-call | flops 3623878656 | bytes 3145728 | tf_op jit(solution)/shard_map/pallas_call | solution.py:325
  55.4 1.4 %slice_bitcast_fusion.1 = f32[32,384]{1,0:T(8,128)} fusion(f32[4,32,384]{2,1,0:T(8,128)} %get-tuple-element.9), kind=kLoop, calls=%fused_computation.2 | loop fusion | bytes 98304 | tf_op jit(solution)/shard_map/squeeze | solution.py:378
  56.8 1.6 %slice_bitcast_fusion = f32[32,3,384]{2,0,1:T(8,128)} fusion(f32[4,32,384]{2,1,0:T(8,128)} %get-tuple-element.9), kind=kLoop, calls=%fused_computation | loop fusion | bytes 294912 | tf_op jit(solution)/shard_map/transpose | solution.py:378
  58.4 0.0 copy-start
  58.4 2.1 %copy.10 = bf16[1,384,1024]{2,1,0:T(8,128)(2,1)} copy(bf16[1,384,1024]{2,1,0:T(8,128)(2,1)} %bitcast.11) | data formatting | bytes 1572864
  60.6 0.0 copy-done
  60.6 0.9 %copy.11 = bf16[1,384,1024]{2,1,0:T(8,128)(2,1)} copy(bf16[1,384,1024]{2,1,0:T(8,128)(2,1)S(1)} %bitcast.10) | data formatting | bytes 1572864
Async XLA Ops:
  58.4 2.1 %copy-start = (bf16[384,1024]{1,0:T(8,128)(2,1)S(1)}, bf16[384,1024]{1,0:T(8,128)(2,1)}, u32[]{:S(2)}) copy-start(bf16[384,1024]{1,0:T(8,128)(2,1)} %get-tuple-element.8) | copy-start | bytes 2359300
